TPU v7x, 32 devices: a whole 2x2x4 slice. The times are simulated.
32 devices in a mesh: patch: 8 (over y, x, core), mlp: 4 (over z).
Axes of the slice: x: 2, y: 2, z: 4, core: 2. Of those that a mesh axis runs over, the one named last changes fastest.
Arguments:
- latent: bfloat16 [2048, 2432], P('patch', 'mlp'), may hold values from -24 to 24
- split_list: int32 [8, 4], P('patch'), may hold values from 0 to 256, as said below
- modulation: float32 [1, 6, 2432], replicated, may hold values from -3 to 3
- w_qkv: bfloat16 [2432, 3, 1536], P(None, None, 'mlp'), may hold values from -0.125 to 0.125
- w_out: bfloat16 [1536, 2432], P('mlp'), may hold values from -0.15625 to 0.15625
- w_up: bfloat16 [2432, 5120], P(None, 'mlp'), may hold values from -0.125 to 0.125
- w_down: bfloat16 [5120, 2432], P('mlp'), may hold values from -0.078125 to 0.078125
- qk_gains: float32 [3, 64], replicated, may hold values from 1.6 to 2.4
- text_kv: bfloat16 [2, 1, 154, 1536], P(None, None, None, 'mlp'), may hold values from -6 to 6
- timestep: int32 [1], replicated, may hold values from 0 to 27
- step_sizes: float32 [28], replicated, may hold values from -0.6 to -0.1
Outputs:
- latent_next: bfloat16 [2048, 2432], P('patch', 'mlp')
Inputs may be any that keep to these rules, and one draw needn't show every extreme that they name: `split_list`: row d holds device d's tile pieces (item, count, item, count); over all devices the counts of every item add up to 1024. A device's two counts add up to at most 256, to exactly 256 on some device and to 0 on another. The devices holding an item's tokens form a run of consecutive indices of patch, taken cyclically. Both pieces may name the same item; they are then two parts of it.
All inputs are finite; a program needn't handle non-finite values.
Results may differ from a plain program's by a relative error of at most 0.0049.
Values may be sent and summed in bfloat16 or wider, within the bound.
A program may use at most 128 MiB of HBM per device.

v0:
```python
import jax
import jax.numpy as jnp
from jax import lax
from jax.sharding import PartitionSpec as P

HEAD = 64
norm_eps = 1e-06
block_rows = 512


def layer_norm(row_data):
    row_mean = jnp.mean(row_data, axis=-1, keepdims=True)
    centred = row_data - row_mean
    variance = jnp.mean(centred * centred, axis=-1, keepdims=True)
    return centred * lax.rsqrt(variance + norm_eps)


def head_norm(row_data, gain_row):
    shaped = row_data.reshape(row_data.shape[0], -1, HEAD)
    mean_square = jnp.mean(shaped * shaped, axis=-1, keepdims=True)
    return (shaped * lax.rsqrt(mean_square + norm_eps) * gain_row).reshape(row_data.shape)


def attend_dense(state_pair, queries, query_tags, key_rows, value_rows, key_tags):
    numerator, denominator = state_pair
    query_count = queries.shape[0]
    heads_here = queries.shape[1] // HEAD
    query_heads = queries.reshape(query_count, heads_here, HEAD)
    key_heads = key_rows.reshape(key_rows.shape[0], heads_here, HEAD)
    value_heads = value_rows.reshape(value_rows.shape[0], heads_here, HEAD)
    scores = jnp.einsum(
        "qhd,khd->qhk", query_heads, key_heads, preferred_element_type=jnp.float32
    ) * HEAD ** (-0.5)
    same_item = (query_tags[:, None] == key_tags[None, :])[:, None, :]
    weights = jnp.where(same_item, jnp.exp(scores), 0.0)
    denominator = denominator + jnp.sum(weights, axis=-1)
    numerator = numerator + jnp.einsum(
        "qhk,khd->qhd",
        weights.astype(jnp.bfloat16),
        value_heads,
        preferred_element_type=jnp.float32,
    )
    return (numerator, denominator)


def attend_block(state_pair, queries, query_tags, key_rows, value_rows, key_tags):
    touching = jnp.any(query_tags[:, None] == key_tags[None, :])

    def work(inner):
        return attend_dense(inner, queries, query_tags, key_rows, value_rows, key_tags)

    def skip(inner):
        return inner

    return lax.cond(touching, work, skip, state_pair)


def attend(state_pair, queries, query_tags, key_rows, value_rows, key_tags):
    key_count = key_rows.shape[0]
    if key_count > 2 * block_rows and key_count % block_rows == 0:

        def one_block(block_index, inner):
            offset = block_index * block_rows
            return attend_block(
                inner,
                queries,
                query_tags,
                lax.dynamic_slice_in_dim(key_rows, offset, block_rows, 0),
                lax.dynamic_slice_in_dim(value_rows, offset, block_rows, 0),
                lax.dynamic_slice_in_dim(key_tags, offset, block_rows, 0),
            )

        return lax.fori_loop(0, key_count // block_rows, one_block, state_pair)
    return attend_block(state_pair, queries, query_tags, key_rows, value_rows, key_tags)


def body(
    latent,
    split_list,
    modulation,
    w_qkv,
    w_out,
    w_up,
    w_down,
    qk_gains,
    text_kv,
    timestep,
    step_sizes,
):
    share_cols = latent.shape[1]
    row_data = lax.all_gather(latent, "mlp", axis=1, tiled=True)
    capacity = row_data.shape[0]
    item_total = modulation.shape[0]
    item_a = split_list[0, 0]
    count_a = split_list[0, 1]
    item_b = split_list[0, 2]
    count_b = split_list[0, 3]
    slot_ids = jnp.arange(capacity, dtype=jnp.int32)
    in_first = slot_ids < count_a
    slot_live = slot_ids < count_a + count_b
    slot_item = jnp.where(in_first, item_a, jnp.where(slot_live, item_b, -1))
    item_ids = jnp.arange(item_total, dtype=jnp.int32)
    one_hot = (slot_item[:, None] == item_ids[None, :]).astype(jnp.float32)
    slot_mods = jnp.dot(
        one_hot,
        modulation.reshape(item_total, -1),
        precision=lax.Precision.HIGHEST,
        preferred_element_type=jnp.float32,
    ).reshape(capacity, 6, -1)
    slot_step = jnp.dot(
        one_hot,
        jnp.take(step_sizes, timestep),
        precision=lax.Precision.HIGHEST,
        preferred_element_type=jnp.float32,
    )
    float_rows = row_data.astype(jnp.float32)
    normed_one = (layer_norm(float_rows) * (1.0 + slot_mods[:, 1]) + slot_mods[:, 0]).astype(
        jnp.bfloat16
    )
    projected = jnp.einsum("nd,dch->nch", normed_one, w_qkv, preferred_element_type=jnp.float32)
    queries = head_norm(projected[:, 0], qk_gains[0]).astype(jnp.bfloat16)
    key_rows = head_norm(projected[:, 1], qk_gains[1]).astype(jnp.bfloat16)
    value_rows = projected[:, 2].astype(jnp.bfloat16)
    head_cols = queries.shape[1]
    heads_here = head_cols // HEAD
    text_pair = jnp.take(text_kv, jnp.stack([item_a, item_b]), axis=1)
    text_keys = head_norm(
        text_pair[0].reshape(-1, head_cols).astype(jnp.float32), qk_gains[2]
    ).astype(jnp.bfloat16)
    text_values = text_pair[1].reshape(-1, head_cols)
    second_tag = jnp.where(item_b != item_a, item_b, -2)
    text_tags = jnp.repeat(jnp.stack([item_a, second_tag]), text_kv.shape[2]).astype(jnp.bfloat16)
    query_tags = slot_item.astype(jnp.bfloat16)
    key_tags = jnp.where(slot_live, slot_item, -3).astype(jnp.bfloat16)
    empty_state = (
        jnp.zeros((capacity, heads_here, HEAD), jnp.float32),
        jnp.zeros((capacity, heads_here), jnp.float32),
    )
    start_state = attend(empty_state, queries, query_tags, text_keys, text_values, text_tags)
    numerator, denominator = attend(
        start_state,
        queries,
        query_tags,
        lax.all_gather(key_rows, "patch", axis=0, tiled=True),
        lax.all_gather(value_rows, "patch", axis=0, tiled=True),
        lax.all_gather(key_tags, "patch", axis=0, tiled=True),
    )
    safe_denominator = denominator + (slot_item < 0).astype(jnp.float32)[:, None]
    attended = (
        (numerator / safe_denominator[:, :, None]).reshape(capacity, head_cols).astype(jnp.bfloat16)
    )
    head_part = jnp.dot(attended, w_out, preferred_element_type=jnp.float32)
    col_first = lax.axis_index("mlp") * share_cols
    attn_total = lax.psum(head_part, "mlp")
    after_attn = float_rows + slot_mods[:, 2] * attn_total
    normed_two = (layer_norm(after_attn) * (1.0 + slot_mods[:, 4]) + slot_mods[:, 3]).astype(
        jnp.bfloat16
    )
    up_total = jnp.dot(normed_two, w_up, preferred_element_type=jnp.float32)
    attn_share = lax.dynamic_slice_in_dim(after_attn, col_first, share_cols, 1)
    hidden_units = jax.nn.gelu(up_total, approximate=True).astype(jnp.bfloat16)
    unit_part = jnp.dot(hidden_units, w_down, preferred_element_type=jnp.float32)
    unit_total = lax.psum_scatter(unit_part, "mlp", scatter_dimension=1, tiled=True)
    gate_share = lax.dynamic_slice_in_dim(slot_mods[:, 5], col_first, share_cols, 1)
    after_mlp = attn_share + gate_share * unit_total
    next_rows = latent.astype(jnp.float32) + slot_step[:, None] * after_mlp
    return jnp.where(slot_live[:, None], next_rows, 0.0).astype(jnp.bfloat16)


def solution(mesh):
    return jax.shard_map(
        body,
        mesh=mesh,
        in_specs=(
            P("patch", "mlp"),
            P("patch", None),
            P(),
            P(None, None, "mlp"),
            P("mlp", None),
            P(None, "mlp"),
            P("mlp", None),
            P(),
            P(None, None, None, "mlp"),
            P(),
            P(),
        ),
        out_specs=P("patch", "mlp"),
        check_vma=False,
    )
```

profile of v0, /device:TPU:0, one launch (start us, length us, event | category | flops | bytes accessed | tf_op | source)
XLA Modules:
  0.0 319.1 jit_solution(8434744912893777445)
XLA Ops:
  13.5 1.9 broadcast_select_fusion.1
  15.4 6.1 %broadcast_multiply_fusion = f32[256,6,2432]{0,2,1:T(8,128)} fusion(f32[6,2432]{1,0:T(8,128)S(1)} %bitcast.153, f32[256]{0:T(256)S(1)} %get-tuple-element.424), kind=kLoop, calls=%fused_computation.23 | loop fusion | flops 3735552 | bytes 15001600 | tf_op jit(solution)/shard_map/dot_general | solution.py:104
  21.6 21.7 %all-gather.6.cloned.1.call-done = bf16[256,2432]{0,1:T(8,128)(2,1)} async-done(((bf16[256,608]{0,1:T(8,128)(2,1)}), bf16[256,2432]{0,1:T(8,128)(2,1)}) %all-gather.6.cloned.1.call-update) | async-done | bytes 1245200 | tf_op jit(solution)/shard_map/all_gather | solution.py:91
  46.7 6.0 %fusion.44 = f32[256,3,384]{2,0,1:T(8,128)S(1)} fusion(bf16[2432,3,384]{2,0,1:T(8,128)(2,1)} %param.20, f32[256,6,2432]{0,2,1:T(8,128)} %broadcast_multiply_fusion, bf16[256,2432]{0,1:T(8,128)(2,1)S(1)} %copy-done.2, f32[256]{0:T(256)S(1)} %add_rsqrt_fusion.4, f32[256]{0:T(256)S(1)} %broadcast_multiply_fusion.2), kind=kOutput, calls=%fused_computation.58 | convolution fusion | flops 1438810112 | bytes 13010944 | tf_op jit(solution)/shard_map/nd,dch->nch/dot_general | solution.py:120
  54.7 2.1 slice_multiply_fusion
  61.2 2.1 fusion.60
  75.1 2.6 reshape.303
  77.7 2.1 copy.113
  79.7 2.2 fusion.63
  81.9 2.6 mul.193
  86.5 2.1 copy.95
  88.7 9.0 %all-gather.1 = bf16[8,1,256]{2,1,0:T(2,128)(2,1)S(1)} all-gather(bf16[1,1,256]{2,1,0:T(2,128)(2,1)S(1)} %reshape.300), channel_id=1, replica_groups=mesh['patch'=8,'mlp'=4] {'patch'}, dimensions={0}, use_global_device_ids=true | all-gather | bytes 4608 | tf_op jit(solution)/shard_map/all_gather | solution.py:146
  100.5 8.4 %conditional.2 = (f32[256,6,64]{0,2,1:T(8,128)S(1)}, f32[256,6]{0,1:T(8,128)S(1)}) conditional(s32[]{:T(128)} %convert_element_type.111, () %tuple.38, (bf16[256]{0:T(256)(128)(2,1)S(1)}, s32[2]{0:T(128)S(1)}, bf16[308,384]{1,0:T(8,128)(2,1)}, bf16[256,384]{1,0:T(8,128)(2,1)S(1)}, bf16[2,2,154,384]{2,1,3,0:T(2,128)(2,1)}) %tuple.110), branch_computations={%region_5.6_spmd, %region_6.8_spmd} | conditional | flops 123080192 | bytes 5880796 | solution.py:55
  100.5 2.0 slice.38
  102.5 2.0 reshape_reshape_squeeze.2
  108.9 2.6 copy.105
  111.5 2.6 copy.103
  114.1 29.6 %while.17 = (s32[]{:T(128)}, f32[256,6,64]{0,2,1:T(8,128)S(1)}, f32[256,6]{0,1:T(8,128)S(1)}, bf16[2048]{0:T(1024)(128)(2,1)S(1)}, bf16[2048,384]{0,1:T(8,128)(2...) while((s32[]{:T(128)}, f32[256,6,64]{0,2,1:T(8,128)S(1)}, ...), condition=%wide.region_14.15_spmd.clone, body=%wide.region_9.14_spmd.clone.sunk | while | flops 206537984 | bytes 10057545 | solution.py:73
  117.6 3.9 %conditional.5 = ((f32[256,6,64]{0,2,1:T(8,128)S(1)}, f32[256,6]{0,1:T(8,128)S(1)})) conditional(s32[]{:T(128)} %convert_element_type.190, (f32[256,6,64]{0,2,1:T(8,128)S(1)}, f32[256,6]{0,1:T(8,128)S(1)}) %tuple.89, (bf16[256]{0:T(256)(128)(2,1)S(1)}, bf16[512]{0:T(512)(128)(2,1)S(1)}, bf16[2048,384]{0,1:T(8,128)(2,1)}, s32[]{:T(128)}, ...), branch_computations={%region_11.11_spmd, %region_12.13_spmd} | conditional | flops 206274560 | bytes 10053148 | solution.py:55
  121.6 1.9 fusion.89
  125.0 3.9 %conditional.5 = ((f32[256,6,64]{0,2,1:T(8,128)S(1)}, f32[256,6]{0,1:T(8,128)S(1)})) conditional(s32[]{:T(128)} %convert_element_type.190, (f32[256,6,64]{0,2,1:T(8,128)S(1)}, f32[256,6]{0,1:T(8,128)S(1)}) %tuple.89, (bf16[256]{0:T(256)(128)(2,1)S(1)}, bf16[512]{0:T(512)(128)(2,1)S(1)}, bf16[2048,384]{0,1:T(8,128)(2,1)}, s32[]{:T(128)}, ...), branch_computations={%region_11.11_spmd, %region_12.13_spmd} | conditional | flops 206274560 | bytes 10053148 | solution.py:55
  129.0 1.9 fusion.89
  132.4 3.9 %conditional.5 = ((f32[256,6,64]{0,2,1:T(8,128)S(1)}, f32[256,6]{0,1:T(8,128)S(1)})) conditional(s32[]{:T(128)} %convert_element_type.190, (f32[256,6,64]{0,2,1:T(8,128)S(1)}, f32[256,6]{0,1:T(8,128)S(1)}) %tuple.89, (bf16[256]{0:T(256)(128)(2,1)S(1)}, bf16[512]{0:T(512)(128)(2,1)S(1)}, bf16[2048,384]{0,1:T(8,128)(2,1)}, s32[]{:T(128)}, ...), branch_computations={%region_11.11_spmd, %region_12.13_spmd} | conditional | flops 206274560 | bytes 10053148 | solution.py:55
  136.4 1.9 fusion.89
  139.8 3.9 %conditional.5 = ((f32[256,6,64]{0,2,1:T(8,128)S(1)}, f32[256,6]{0,1:T(8,128)S(1)})) conditional(s32[]{:T(128)} %convert_element_type.190, (f32[256,6,64]{0,2,1:T(8,128)S(1)}, f32[256,6]{0,1:T(8,128)S(1)}) %tuple.89, (bf16[256]{0:T(256)(128)(2,1)S(1)}, bf16[512]{0:T(512)(128)(2,1)S(1)}, bf16[2048,384]{0,1:T(8,128)(2,1)}, s32[]{:T(128)}, ...), branch_computations={%region_11.11_spmd, %region_12.13_spmd} | conditional | flops 206274560 | bytes 10053148 | solution.py:55
  143.8 2.4 fusion.75
  146.3 98.0 %all-reduce.2.cloned.1.call-done = f32[256,2432]{0,1:T(8,128)} async-done(((f32[256,2432]{0,1:T(8,128)}), f32[256,2432]{0,1:T(8,128)}) %all-reduce.2.cloned.1.call-update) | async-done | bytes 2490384 | tf_op jit(solution)/shard_map/psum | solution.py:154
  244.3 2.9 fusion.71
  249.0 12.0 %convolution_bitcast_fusion.1 = f32[2432,256]{1,0:T(8,128)} fusion(bf16[1280,2432]{1,0:T(8,128)(2,1)} %param.23, bf16[2432,1280]{1,0:T(8,128)(2,1)} %param.22, f32[256,6,2432]{0,2,1:T(8,128)} %broadcast_multiply_fusion, f32[256,2432]{0,1:T(8,128)} %copy-done.1, f32[256]{0:T(256)S(1)} %add_rsqrt_fusion.3, f32[256]{0:T(256)S(1)} %broadcast_multiply_fusion.1), kind=kOutput, calls=%fused_computation.24 | convolution fusion | flops 3194355712 | bytes 22415360
  261.0 3.4 %slice.85 = f32[256,1,2432]{0,2,1:T(8,128)} slice(f32[256,6,2432]{0,2,1:T(8,128)} %broadcast_multiply_fusion), slice={[0:256], [5:6], [0:2432]} | slice | bytes 4980736 | tf_op jit(solution)/shard_map/slice | solution.py:164
  264.4 45.9 %reduce-scatter.4.cloned.1.call-done = f32[608,256]{1,0:T(8,128)} async-done(((f32[2432,256]{1,0:T(8,128)}), f32[608,256]{1,0:T(8,128)}) %reduce-scatter.4.cloned.1.call-update) | async-done | bytes 622608
  310.3 2.3 fusion.58
  (114 shorter events, 55.0 us)
Async XLA Ops:
  6.5 137.3 %copy-start = (bf16[384,2432]{1,0:T(8,128)(2,1)S(1)}, bf16[384,2432]{1,0:T(8,128)(2,1)}, u32[]{:S(2)}) copy-start(bf16[384,2432]{1,0:T(8,128)(2,1)} %param.21) | copy-start | bytes 5603332
  6.5 36.7 %all-gather.6.cloned.1.call-start = ((), (), s32[]{:S(2)}) async-start(), calls=%async_computation.1 | async-start | bytes 1556480 | tf_op jit(solution)/shard_map/all_gather | solution.py:91
  7.3 101.7 %all-gather.10.cloned.1.call-start = ((), (), s32[]{:S(2)}) async-start(), calls=%async_computation.4 | async-start | bytes 1769472 | tf_op jit(solution)/shard_map/all_gather | solution.py:145
  43.2 3.4 %copy-start.2 = (bf16[256,2432]{0,1:T(8,128)(2,1)S(1)}, bf16[256,2432]{0,1:T(8,128)(2,1)}, u32[]{:S(2)}) copy-start(bf16[256,2432]{0,1:T(8,128)(2,1)} %all-gather.6.cloned.1.call-done) | copy-start | bytes 3735556
  46.7 7.9 %copy-start.7 = (f32[3,64]{1,0:T(4,128)S(1)}, f32[3,64]{1,0:T(4,128)}, u32[]{:S(2)}) copy-start(f32[3,64]{1,0:T(4,128)} %param.24) | copy-start | bytes 2308
  52.7 1.0 copy-start.4
  54.5 57.1 %all-gather.8.cloned.1.call-start = ((), (), s32[]{:S(2)}) async-start(), calls=%async_computation.2 | async-start | bytes 1769472 | tf_op jit(solution)/shard_map/all_gather | solution.py:144
  63.3 181.0 %all-reduce.2.cloned.1.call-start = ((), (), s32[]{:S(2)}) async-start(), calls=%async_computation.3 | async-start | bytes 4980736 | tf_op jit(solution)/shard_map/psum | solution.py:154
  72.9 0.9 copy-start.3
  106.6 1.7 copy-start.6
  146.3 164.0 %reduce-scatter.4.cloned.1.call-start = ((), (), s32[]{:S(2)}) async-start(), calls=%async_computation.5 | async-start | bytes 3112960
  247.2 1.4 copy-start.1
  261.0 49.3 %copy-start.5 = (bf16[256,608]{0,1:T(8,128)(2,1)S(1)}, bf16[256,608]{0,1:T(8,128)(2,1)}, u32[]{:S(2)}) copy-start(bf16[256,608]{0,1:T(8,128)(2,1)} %param.17) | copy-start | bytes 933892
Sparse Core Ops, SparseCore 0:
  8.9 34.2 all-gather.5
  54.6 24.7 all-gather.9
  81.3 25.7 all-gather.7
  146.4 97.8 all-reduce.1
  261.1 49.0 reduce-scatter.3
where the time goes:
time: 321 us; the launch traced here: 319 us
  waiting for transfers between devices  166 us (52%)
  local copies, waits for them, and re-layouts  45.1 us (14%)
  other arithmetic  44.3 us (14%)
  matrix products  32.5 us (10%)
  between operations  18.6 us (6%)
  blocking collectives  9.01 us (3%)
    psum x1, waiting for transfers between devices, body(): attn_total = lax.psum(head_part, 'mlp')  98 us
    unnamed x6, waiting for transfers between devices  46.6 us
    all_gather x1, waiting for transfers between devices, body(): row_data = lax.all_gather(latent, 'mlp', axis=1, tiled=True)  21.7 us
    unnamed x1, matrix products  12 us
    unnamed x20, local copies, waits for them, and re-layouts  10.3 us
    all_gather x1, blocking collectives, body(): lax.all_gather(key_tags, 'patch', axis=0, tiled=True)  9.01 us
    dot_general x5, matrix products, attend_dense(): jnp.einsum('qhd,khd->qhk', query_heads, key_heads, preferred_element_type...  8.96 us
    convert_element_type x4, other arithmetic, body(): query_tags = slot_item.astype(jnp.bfloat16)  7.74 us
  transfers between devices with their start and end apart: 5, of which 3 were waited for; matrix products, arithmetic and copies ran while one was open for 18% of the time, Pallas kernels for 0%

commit v1 on v0

--- a/solution.py
+++ b/solution.py
@@ -151,7 +151,8 @@
     )
     head_part = jnp.dot(attended, w_out, preferred_element_type=jnp.float32)
     col_first = lax.axis_index("mlp") * share_cols
-    attn_total = lax.psum(head_part, "mlp")
+    parts = lax.all_gather(head_part, "mlp")
+    attn_total = jnp.sum(parts, axis=0)
     after_attn = float_rows + slot_mods[:, 2] * attn_total
     normed_two = (layer_norm(after_attn) * (1.0 + slot_mods[:, 4]) + slot_mods[:, 3]).astype(
         jnp.bfloat16

time: 321 us -> 403 us (1.26)
  waiting for transfers between devices: 166 us -> 241 us
  other arithmetic: 44.3 us -> 49.9 us
    all_gather x0 -> x1, waiting for transfers between devices: none -> 174 us  [body(): parts = lax.all_gather(head_part, 'mlp')]
    psum x1 -> x0, waiting for transfers between devices: 98 us -> none  [body(): attn_total = lax.psum(head_part, 'mlp')]
    unnamed x6 -> x5, waiting for transfers between devices: 46.6 us -> 0.78 us
    reduce_scatter x0 -> x1, waiting for transfers between devices: none -> 45 us  [body(): lax.psum_scatter(unit_part, 'mlp', scatter_dimension=1, tiled=True)]
    unnamed x1 -> x0, matrix products: 12 us -> none
    dot_general x0 -> x1, matrix products: none -> 12 us  [body(): jnp.dot(hidden_units, w_down, preferred_element_type=jnp.float32)]
    reduce_sum x0 -> x1, other arithmetic: none -> 6.14 us  [body(): attn_total = jnp.sum(parts, axis=0)]
  transfers between devices with their start and end apart: 5 -> 5, of which waited for: 3 -> 3; matrix products, arithmetic and copies ran while one was open for 18% -> 15% of each run, Pallas kernels for 0% -> 0%
where the time goes in v1:
time: 403 us; the launch traced here: 402 us
  waiting for transfers between devices  241 us (60%)
  other arithmetic  49.9 us (12%)
  local copies, waits for them, and re-layouts  45.4 us (11%)
  matrix products  34.7 us (9%)
  between operations  18.5 us (5%)
  blocking collectives  8.89 us (2%)
    all_gather x1, waiting for transfers between devices, body(): parts = lax.all_gather(head_part, 'mlp')  174 us
    reduce_scatter x1, waiting for transfers between devices, body(): lax.psum_scatter(unit_part, 'mlp', scatter_dimension=1, tiled=True)  45 us
    all_gather x1, waiting for transfers between devices, body(): row_data = lax.all_gather(latent, 'mlp', axis=1, tiled=True)  21.9 us
    dot_general x1, matrix products, body(): jnp.dot(hidden_units, w_down, preferred_element_type=jnp.float32)  12 us
    unnamed x20, local copies, waits for them, and re-layouts  10.2 us
    dot_general x5, matrix products, attend_dense(): jnp.einsum('qhd,khd->qhk', query_heads, key_heads, preferred_element_type...  9.97 us
    all_gather x1, blocking collectives, body(): lax.all_gather(key_tags, 'patch', axis=0, tiled=True)  8.89 us
  transfers between devices with their start and end apart: 5, of which 3 were waited for; matrix products, arithmetic and copies ran while one was open for 15% of the time, Pallas kernels for 0%

profile of v1, /device:TPU:0, one launch (start us, length us, event | category | flops | bytes accessed | tf_op | source)
XLA Modules:
  0.0 401.8 jit_solution(10094006613317877785)
XLA Ops:
  15.2 6.1 %broadcast_multiply_fusion = f32[256,6,2432]{0,2,1:T(8,128)} fusion(f32[6,2432]{1,0:T(8,128)S(1)} %bitcast.151, f32[256]{0:T(256)S(1)} %get-tuple-element.408), kind=kLoop, calls=%fused_computation.23 | loop fusion | flops 3735552 | bytes 15001600 | tf_op jit(solution)/shard_map/dot_general | solution.py:104
  21.4 21.9 %all-gather.8.cloned.1.call-done = bf16[256,2432]{0,1:T(8,128)(2,1)} async-done(((bf16[256,608]{0,1:T(8,128)(2,1)}), bf16[256,2432]{0,1:T(8,128)(2,1)}) %all-gather.8.cloned.1.call-update) | async-done | bytes 1245200 | tf_op jit(solution)/shard_map/all_gather | solution.py:91
  46.7 6.0 %fusion.44 = f32[256,3,384]{2,0,1:T(8,128)S(1)} fusion(bf16[2432,3,384]{2,0,1:T(8,128)(2,1)} %param.20, f32[256,6,2432]{0,2,1:T(8,128)} %broadcast_multiply_fusion, bf16[256,2432]{0,1:T(8,128)(2,1)S(1)} %copy-done.2, f32[256]{0:T(256)S(1)} %add_rsqrt_fusion.4, f32[256]{0:T(256)S(1)} %broadcast_multiply_fusion.2), kind=kOutput, calls=%fused_computation.57 | convolution fusion | flops 1438810112 | bytes 13010944 | tf_op jit(solution)/shard_map/nd,dch->nch/dot_general | solution.py:120
  54.7 2.1 slice_multiply_fusion
  61.1 2.1 fusion.61
  64.7 1.9 copy.65
  71.9 2.6 mul.193
  76.5 2.1 copy.67
  78.6 2.2 slice_convert_fusion.1
  80.8 2.6 reshape.304
  83.4 2.1 copy.81
  88.6 8.9 %all-gather.2 = bf16[8,1,256]{2,1,0:T(2,128)(2,1)S(1)} all-gather(bf16[1,1,256]{2,1,0:T(2,128)(2,1)S(1)} %reshape.301), channel_id=1, replica_groups=mesh['patch'=8,'mlp'=4] {'patch'}, dimensions={0}, use_global_device_ids=true | all-gather | bytes 4608 | tf_op jit(solution)/shard_map/all_gather | solution.py:146
  97.5 1.9 multiply_convert_fusion
  100.2 7.9 %conditional.2 = (f32[256,6,64]{0,2,1:T(8,128)S(1)}, f32[256,6]{0,1:T(8,128)S(1)}) conditional(s32[]{:T(128)} %convert_element_type.111, () %tuple.38, (bf16[256]{0:T(256)(128)(2,1)S(1)}, s32[2]{0:T(128)S(1)}, bf16[308,384]{1,0:T(8,128)(2,1)}, bf16[256,384]{1,0:T(8,128)(2,1)S(1)}, bf16[2,2,154,384]{2,1,3,0:T(2,128)(2,1)}) %tuple.108), branch_computations={%region_5.6_spmd, %region_6.8_spmd} | conditional | flops 123080192 | bytes 6826972 | solution.py:55
  102.5 2.7 fusion.74
  108.2 2.6 copy.77
  110.8 2.6 copy.75
  113.4 28.8 %while.17 = (s32[]{:T(128)}, f32[256,6,64]{0,2,1:T(8,128)S(1)}, f32[256,6]{0,1:T(8,128)S(1)}, bf16[2048]{0:T(1024)(128)(2,1)S(1)}, bf16[2048,384]{0,1:T(8,128)(2...) while((s32[]{:T(128)}, f32[256,6,64]{0,2,1:T(8,128)S(1)}, ...), condition=%wide.region_14.15_spmd.clone, body=%wide.region_9.14_spmd.clone.sunk | while | flops 206537984 | bytes 10057537 | solution.py:73
  116.7 3.9 conditional.5
  120.7 1.9 fusion.90
  123.9 3.9 conditional.5
  131.1 3.9 conditional.5
  138.3 3.9 conditional.5
  142.3 2.4 fusion.76
  144.7 173.8 %all-gather.14.cloned.1.call-done = f32[1024,2432]{1,0:T(8,128)} async-done(((f32[256,2432]{1,0:T(8,128)}), f32[1024,2432]{1,0:T(8,128)}) %all-gather.14.cloned.1.call-update) | async-done | bytes 9961488 | tf_op jit(solution)/shard_map/all_gather | solution.py:154
  318.5 6.1 %reduce_sum.97 = f32[256,2432]{1,0:T(8,128)} reduce(f32[4,256,2432]{2,1,0:T(8,128)} %bitcast.142, f32[]{:T(128)} %constant.118.clone.1), dimensions={0}, to_apply=%region_15.16 | reduce | flops 1867776 | bytes 12451844 | tf_op jit(solution)/shard_map/reduce_sum | solution.py:155
  324.7 3.2 copy.78
  327.9 2.9 fusion.72
  332.5 12.0 %fusion.53 = f32[256,2432]{0,1:T(8,128)} fusion(bf16[1280,2432]{1,0:T(8,128)(2,1)} %param.23, bf16[2432,1280]{1,0:T(8,128)(2,1)} %param.22, f32[256,6,2432]{0,2,1:T(8,128)} %broadcast_multiply_fusion, f32[256,2432]{0,1:T(8,128)} %copy-done.1, f32[256]{0:T(256)S(1)} %add_rsqrt_fusion.3, f32[256]{0:T(256)S(1)} %broadcast_multiply_fusion.1), kind=kOutput, calls=%fused_computation.64 | convolution fusion | flops 3194355712 | bytes 22415360 | tf_op jit(solution)/shard_map/dot_general | solution.py:163
  344.6 3.4 slice.85
  348.0 45.0 %reduce-scatter.2.cloned.1.call-done = f32[256,608]{0,1:T(8,128)} async-done(((f32[256,2432]{0,1:T(8,128)}), f32[256,608]{0,1:T(8,128)}) %reduce-scatter.2.cloned.1.call-update) | async-done | bytes 622608 | tf_op jit(solution)/shard_map/reduce_scatter | solution.py:164
  393.0 2.3 fusion.59
  (116 shorter events, 57.2 us)
Async XLA Ops:
  6.5 135.8 %copy-start = (bf16[384,2432]{1,0:T(8,128)(2,1)S(1)}, bf16[384,2432]{1,0:T(8,128)(2,1)}, u32[]{:S(2)}) copy-start(bf16[384,2432]{1,0:T(8,128)(2,1)} %param.21) | copy-start | bytes 5603332
  6.5 36.7 %all-gather.8.cloned.1.call-start = ((), (), s32[]{:S(2)}) async-start(), calls=%async_computation.1 | async-start | bytes 1556480 | tf_op jit(solution)/shard_map/all_gather | solution.py:91
  7.3 100.9 %all-gather.12.cloned.1.call-start = ((), (), s32[]{:S(2)}) async-start(), calls=%async_computation.4 | async-start | bytes 1769472 | tf_op jit(solution)/shard_map/all_gather | solution.py:145
  43.2 3.4 copy-start.2
  46.7 7.9 %copy-start.7 = (f32[3,64]{1,0:T(4,128)S(1)}, f32[3,64]{1,0:T(4,128)}, u32[]{:S(2)}) copy-start(f32[3,64]{1,0:T(4,128)} %param.24) | copy-start | bytes 2308
  52.7 1.0 copy-start.5
  54.5 56.3 %all-gather.10.cloned.1.call-start = ((), (), s32[]{:S(2)}) async-start(), calls=%async_computation.2 | async-start | bytes 1769472 | tf_op jit(solution)/shard_map/all_gather | solution.py:144
  63.3 255.2 %all-gather.14.cloned.1.call-start = ((), (), s32[]{:S(2)}) async-start(), calls=%async_computation.5 | async-start | bytes 12451840 | tf_op jit(solution)/shard_map/all_gather | solution.py:154
  69.8 0.9 copy-start.3
  102.4 2.8 copy-start.4
  144.7 248.3 %reduce-scatter.2.cloned.1.call-start = ((), (), s32[]{:S(2)}) async-start(), calls=%async_computation.3 | async-start | bytes 3112960 | tf_op jit(solution)/shard_map/reduce_scatter | solution.py:164
  330.7 1.4 copy-start.1
  344.6 48.4 %copy-start.6 = (bf16[256,608]{0,1:T(8,128)(2,1)S(1)}, bf16[256,608]{0,1:T(8,128)(2,1)}, u32[]{:S(2)}) copy-start(bf16[256,608]{0,1:T(8,128)(2,1)} %param.17) | copy-start | bytes 933892
Sparse Core Ops, SparseCore 0:
  8.9 34.2 all-gather.7
  54.6 24.7 all-gather.11
  81.3 25.7 all-gather.9
  144.8 173.6 all-gather.13
  344.7 48.2 reduce-scatter.1
